TPU v7x, 512 devices: a whole 4x4x16 slice. The times are simulated.
512 devices in a mesh: sec: 4 (over z_hi, core), gx: 32 (over y, z_lo), gy: 4 (over x).
Axes of the slice: x: 4, y: 4, z: 16 (z_hi: 2, z_lo: 8; z = z_hi * 8 + z_lo), core: 2. Of those that a mesh axis runs over, the one named last changes fastest.
Arguments:
- adjoint: float32 [4, 5, 256, 32, 128], P('sec', None, 'gx', 'gy'), may hold values from -6 to 6
- flow: float32 [4, 6, 256, 32, 128], P('sec', None, 'gx', 'gy'), as said below
- point_cell: int32 [4, 32, 4, 1024], P('sec', 'gx', 'gy'), may hold values from 0 to 8191
- point_dest: int32 [4, 32, 4, 1024], P('sec', 'gx', 'gy'), may hold values from 0 to 127, as said below
- point_target: int32 [4, 32, 4, 1024], P('sec', 'gx', 'gy'), may hold values from 0 to 8191
- point_weight: float32 [4, 32, 4, 1024], P('sec', 'gx', 'gy'), may hold values from 0.5 to 2
- point_count: int32 [4, 32, 4], P('sec', 'gx', 'gy'), may hold values from 0 to 1024, as said below
Outputs:
- adjoint_next: float32 [4, 5, 256, 32, 128], P('sec', None, 'gx', 'gy')
Inputs may be any that keep to these rules, and one draw needn't show every extreme that they name: `flow`: density 0.6 to 1.6, pressure 0.4 (E - kinetic) from 0.5 to 1.5, sponge rate 0.05 to 1. `point_count`: zero on the near-field section; on far-field tiles a multiple of 128, reaching 1024 on some tile. `point_dest`: among the live slots of one far-field tile at most 20 name the same near-field tile, and 20 is reached. Near-field tiles receive unequal numbers of points.
All inputs are finite; a program needn't handle non-finite values.
Results may differ from a plain program's by a relative error of at most 0.00002.
Values sent between devices are 32-bit elements; how exact they have to be, the bound alone decides.
A program may use at most 64 MiB of HBM per device.

v0:
```python
import jax
import jax.numpy as jnp
from jax import lax
from jax.sharding import PartitionSpec as P

GAMMA_MINUS = 0.4
GAMMA_RATIO = 1.4
STEP_SIZE = 0.4


def extended(x, sides, width):
    for axis, dim in sides:
        count, length = (lax.axis_size(axis), x.shape[dim])
        up = [(i, (i + 1) % count) for i in range(count - 1)]
        down = [(j, i) for i, j in up]
        last = lax.slice_in_dim(x, length - width, length, axis=dim)
        initial = lax.slice_in_dim(x, 0, width, axis=dim)
        before = lax.ppermute(last, axis, up)
        after = lax.ppermute(initial, axis, down)
        x = jnp.concatenate([before, x, after], axis=dim)
    return x


def shifted(padded, offset, along):
    length = padded.shape[along] - 6
    return lax.slice_in_dim(padded, 3 + offset, 3 + offset + length, axis=along)


def stencil(padded, along):
    first = shifted(padded, 1, along) - shifted(padded, -1, along)
    second = shifted(padded, 2, along) - shifted(padded, -2, along)
    third = shifted(padded, 3, along) - shifted(padded, -3, along)
    return (45.0 * first - 9.0 * second + third) / 60.0


def wrap_last(values_in):
    return jnp.concatenate([values_in[..., -3:], values_in, values_in[..., :3]], axis=-1)


def fluxes(adjoint, flow, direction):
    density = flow[0]
    inverse = 1.0 / density
    momenta = flow[1:4]
    velocity = momenta[direction] * inverse
    kinetic = (
        0.5
        * (momenta[0] * momenta[0] + momenta[1] * momenta[1] + momenta[2] * momenta[2])
        * inverse
    )
    pressure = GAMMA_MINUS * (flow[4] - kinetic)
    stiffness = GAMMA_RATIO * pressure
    return jnp.stack(
        [
            velocity * adjoint[0],
            velocity * adjoint[1],
            velocity * adjoint[2],
            velocity * adjoint[3],
            velocity * adjoint[4],
            density * adjoint[0] + stiffness * adjoint[4],
            adjoint[1 + direction] * inverse,
        ]
    )


def masked_fluxes(adjoint, flow, direction, inside):
    safe_flow = jnp.concatenate([jnp.where(inside, flow[:1], 1.0), flow[1:]], axis=0)
    return jnp.where(inside, fluxes(adjoint, safe_flow, direction), 0.0)


def assemble(adjoint, flow, along_x, along_y, along_z, source):
    summed = along_x + along_y + along_z
    rate_list = jnp.stack(
        [
            summed[0],
            summed[1] + along_x[5],
            summed[2] + along_y[5],
            summed[3] + along_z[5],
            summed[4] + summed[6],
        ]
    )
    return adjoint + STEP_SIZE * (rate_list - flow[5] * adjoint + source)


def local(adjoint, flow, point_cell, point_dest, point_target, point_weight, point_count):
    adjoint_block = adjoint[0]
    fields = flow[0]
    channels, rows_x, rows_y, depth_cells = adjoint_block.shape
    tile_count = lax.axis_size("gx") * lax.axis_size("gy")
    slot_count = point_cell.shape[-1]
    capacity = 5 * slot_count // (2 * tile_count)
    buffer_width = tile_count * capacity
    cell_index = point_cell.reshape(slot_count)
    dest_tile = point_dest.reshape(slot_count)
    target_cell = point_target.reshape(slot_count)
    flat_block = adjoint_block.reshape(channels, -1)
    values = flat_block[:, cell_index] * point_weight.reshape(slot_count)[None, :]
    live_slot = jnp.arange(slot_count, dtype=jnp.int32) < point_count.reshape(())
    onehot = (
        (dest_tile[:, None] == jnp.arange(tile_count, dtype=jnp.int32)[None, :])
        & live_slot[:, None]
    ).astype(jnp.int32)
    slot_rank = jnp.sum(jnp.cumsum(onehot, axis=0) * onehot, axis=1) - 1
    position = jnp.where(live_slot, dest_tile * capacity + slot_rank, buffer_width)
    packed_values = (
        jnp.zeros((channels, buffer_width), jnp.float32).at[:, position].set(values, mode="drop")
    )
    packed_targets = (
        jnp.zeros((1, buffer_width), jnp.int32).at[0, position].set(target_cell, mode="drop")
    )
    tile_values, tile_targets = (
        lax.all_to_all(packed_values, ("gx", "gy"), split_axis=1, concat_axis=1, tiled=True),
        lax.all_to_all(packed_targets, ("gx", "gy"), split_axis=1, concat_axis=1, tiled=True),
    )
    merged_values, merged_targets = (
        lax.all_gather(tile_values, "sec", axis=1, tiled=True),
        lax.all_gather(tile_targets, "sec", axis=1, tiled=True),
    )
    source = jnp.zeros((channels, rows_x * rows_y * depth_cells), jnp.float32)
    source = (
        source.at[:, merged_targets[0]]
        .add(merged_values)
        .reshape(channels, rows_x, rows_y, depth_cells)
    )
    is_near = lax.axis_index("sec") == lax.axis_size("sec") - 1
    source = jnp.where(is_near, source, 0.0)
    joined = jnp.concatenate([adjoint_block, fields], axis=0)
    padded = extended(joined, (("gx", 1), ("gy", 2)), 3)
    x_position = lax.axis_index("gx") * rows_x - 3 + jnp.arange(rows_x + 6, dtype=jnp.int32)
    x_inside = (x_position >= 0) & (x_position < lax.axis_size("gx") * rows_x)
    y_position = lax.axis_index("gy") * rows_y - 3 + jnp.arange(rows_y + 6, dtype=jnp.int32)
    y_inside = (y_position >= 0) & (y_position < lax.axis_size("gy") * rows_y)
    strip_x = padded[:, :, 3:-3, :]
    flux_x = masked_fluxes(strip_x[:channels], strip_x[channels:], 0, x_inside[:, None, None])
    along_x = stencil(flux_x, 1)
    strip_y = padded[:, 3:-3, :, :]
    flux_y = masked_fluxes(strip_y[:channels], strip_y[channels:], 1, y_inside[None, :, None])
    along_y = stencil(flux_y, 2)
    along_z = stencil(wrap_last(fluxes(adjoint_block, fields, 2)), 3)
    result = assemble(adjoint_block, fields, along_x, along_y, along_z, source)
    return result[None]


def solution(mesh):
    placed = (
        P("sec", None, "gx", "gy", None),
        P("sec", None, "gx", "gy", None),
        P("sec", "gx", "gy", None),
        P("sec", "gx", "gy", None),
        P("sec", "gx", "gy", None),
        P("sec", "gx", "gy", None),
        P("sec", "gx", "gy"),
    )
    return jax.shard_map(
        local,
        mesh=mesh,
        in_specs=placed,
        out_specs=P("sec", None, "gx", "gy", None),
        check_vma=False,
    )
```

profile of v0, /device:TPU:91, one launch (start us, length us, event | category | flops | bytes accessed | tf_op | source)
XLA Modules:
  0.0 204.8 jit_solution(14550307588079525748)
XLA Ops:
  0.0 0.8 copy.17
  1.5 0.3 fusion.6
  2.1 1.2 fusion.4
  3.3 0.7 compare_select_fusion.2
  4.0 0.8 and_reduce_fusion
  4.8 0.7 fusion.72
  5.6 4.5 %scatter_custom_fusion.2 = s32[2560]{0:T(1024)S(1)} fusion(s32[1024]{0:T(1024)S(1)} %broadcast_select_fusion.3, s32[1024]{0:T(1024)} %bitcast.146, s32[]{:T(128)} %constant.27.clone.1), kind=kCustom, calls=%fused_computation.167 | custom fusion | bytes 10752
  10.0 0.7 all_to_all.16
  10.8 18.3 %all-to-all-start = ((s32[1,128,20]{2,0,1:T(1,128)}), s32[1,128,20]{2,0,1:T(1,128)S(1)}, u32[]{:S(2)}, u32[]{:S(2)}) async-start(s32[1,128,20]{2,0,1:T(1,128)} %bitcast.26), calls=%async_computation | async-start | bytes 131072 | tf_op jit(solution)/shard_map/all_to_all | solution.py:112
  29.1 1.6 pad_maximum_fusion.4
  30.7 2.2 %collective-permute-start.1 = (f32[11,3,8,128]{3,2,1,0:T(8,128)}, f32[11,3,8,128]{3,2,1,0:T(8,128)S(1)}, u32[]{:S(2)}, u32[]{:S(2)}) collective-permute-start(f32[11,3,8,128]{3,2,1,0:T(8,128)} %get-tuple-element.18), channel_id=1, source_target_pairs={{4,0},{8,4},{12,8},{16,12},{20,16},{24,20},{28,24},{32,28},{36,32}... | collective-permute-start | bytes 405512 | tf_op jit(solution)/shard_map/ppermute | solution.py:19
  32.8 3.1 %collective-permute-start = (f32[11,3,8,128]{3,2,1,0:T(8,128)S(1)}, f32[11,3,8,128]{3,2,1,0:T(8,128)S(1)}, u32[]{:S(2)}, u32[]{:S(2)}) collective-permute-start(f32[11,3,8,128]{3,2,1,0:T(8,128)S(1)} %get-tuple-element.17), channel_id=1, source_target_pairs={{0,4},{4,8},{8,12},{12,16},{16,20},{20,24},{24,28},{28,32},{32,36}... | collective-permute-start | bytes 405512 | tf_op jit(solution)/shard_map/ppermute | solution.py:18
  36.3 2.7 %copy.20 = f32[1,5,8,8,128]{1,4,3,2,0:T(8,128)} copy(f32[1,5,8,8,128]{4,3,2,1,0:T(8,128)S(1)} %copy-done) | data formatting | bytes 327680 | tf_op args[0]
  39.0 9.7 %scatter_custom_fusion = f32[5,2560]{0,1:T(8,128)S(1)} fusion(s32[1024]{0:T(1024)S(1)} %bitcast.142, f32[]{:T(128)} %constant.32.clone.1, f32[1024]{0:T(1024)S(1)} %bitcast.145, f32[5,8192]{0,1:T(8,128)} %bitcast.136, s32[1024]{0:T(1024)S(1)} %broadcast_clamp_fusion), kind=kCustom, calls=%fused_computation.7 | custom fusion | flops 5120 | bytes 223236 | tf_op jit(solution)/shard_map/scatter | solution.py:105
  48.7 0.4 copy.21
  49.1 0.4 all_to_all.19
  49.5 1.0 copy.22
  50.5 23.5 %all-to-all-start.1 = ((f32[5,128,20]{2,0,1:T(8,128)}), f32[5,128,20]{2,0,1:T(8,128)S(1)}, u32[]{:S(2)}, u32[]{:S(2)}) async-start(f32[5,128,20]{2,0,1:T(8,128)} %copy.22), calls=%async_computation.1 | async-start | bytes 1048576 | tf_op jit(solution)/shard_map/all_to_all | solution.py:111
  74.0 0.6 broadcast.293
  74.6 0.8 reduce.7
  75.6 27.9 %all_gather.6 = s32[1,10240]{1,0:T(1,128)S(1)} all-gather(s32[1,2560]{1,0:T(1,128)S(1)} %all_to_all.18), channel_id=1, replica_groups=mesh['sec'=4,'gx'=32,'gy'=4] {'sec'}, dimensions={1}, use_global_device_ids=true | all-gather | bytes 51200 | tf_op jit(solution)/shard_map/all_gather | solution.py:116
  103.6 0.9 fusion.80
  104.5 2.2 %collective-permute-start.3 = (f32[11,14,3,128]{3,2,1,0:T(4,128)}, f32[11,14,3,128]{3,2,1,0:T(4,128)S(1)}, u32[]{:S(2)}, u32[]{:S(2)}) collective-permute-start(f32[11,14,3,128]{3,2,1,0:T(4,128)} %get-tuple-element.16), channel_id=1, source_target_pairs={{1,0},{2,1},{3,2},{5,4},{6,5},{7,6},{9,8},{10,9},{11,10},{13,12},{... | collective-permute-start | bytes 709640 | tf_op jit(solution)/shard_map/ppermute | solution.py:19
  106.7 3.3 %collective-permute-start.2 = (f32[11,14,3,128]{3,2,1,0:T(4,128)}, f32[11,14,3,128]{3,2,1,0:T(4,128)S(1)}, u32[]{:S(2)}, u32[]{:S(2)}) collective-permute-start(f32[11,14,3,128]{3,2,1,0:T(4,128)} %get-tuple-element.15), channel_id=1, source_target_pairs={{0,1},{1,2},{2,3},{4,5},{5,6},{6,7},{8,9},{9,10},{10,11},{12,13},{... | collective-permute-start | bytes 709640 | tf_op jit(solution)/shard_map/ppermute | solution.py:18
  110.5 0.2 all_to_all.21
  110.8 17.0 %all_gather.7 = f32[5,10240]{1,0:T(8,128)S(1)} all-gather(f32[5,2560]{1,0:T(8,128)S(1)} %all_to_all.21), channel_id=1, replica_groups=mesh['sec'=4,'gx'=32,'gy'=4] {'sec'}, dimensions={1}, use_global_device_ids=true | all-gather | bytes 256000 | tf_op jit(solution)/shard_map/all_gather | solution.py:115
  127.7 3.1 %copy.24 = f32[10240,5]{1,0:T(8,128)} copy(f32[10240,5]{0,1:T(8,128)S(1)} %bitcast.138) | data formatting | bytes 409600 | tf_op jit(solution)/shard_map/all_gather | solution.py:115
  130.9 66.5 %scatter_custom_fusion.1 = f32[5,8192]{0,1:T(8,128)} fusion(s32[10240]{0:T(1024)S(1)} %bitcast.139, f32[10240,5]{1,0:T(8,128)} %copy.24, f32[]{:T(128)} %constant.32.clone.1), kind=kCustom, calls=%fused_computation.5 | custom fusion | flops 51200 | bytes 164352 | tf_op jit(solution)/shard_map/scatter-add | solution.py:121
  197.3 2.3 %broadcast_select_fusion = f32[5,8192]{0,1:T(8,128)} fusion(f32[5,8192]{0,1:T(8,128)} %scatter_custom_fusion.1, pred[]{:T(512)S(6)} %eq.28), kind=kLoop, calls=%fused_computation.4 | loop fusion | flops 40960 | bytes 327681 | tf_op jit(solution)/shard_map/jit(_where)/select_n | solution.py:125
  199.6 2.9 %copy.25 = f32[1,5,8,8,128]{4,3,2,1,0:T(8,128)S(1)} copy(f32[1,5,8,8,128]{1,4,3,2,0:T(8,128)} %bitcast.137) | data formatting | bytes 327680 | tf_op jit(solution)/shard_map/jit(_where)/select_n | solution.py:125
  203.3 0.7 add_add_fusion
  204.1 0.7 multiply_add_fusion
  (61 shorter events, 2.0 us)
Async XLA Ops:
  0.0 36.0 %copy-start.1 = (f32[1,6,8,8,128]{4,3,2,1,0:T(8,128)S(1)}, f32[1,6,8,8,128]{4,3,2,1,0:T(8,128)}, u32[]{:S(2)}) copy-start(f32[1,6,8,8,128]{4,3,2,1,0:T(8,128)} %param.8) | copy-start | bytes 589828
  0.0 36.0 %copy-start = (f32[1,5,8,8,128]{4,3,2,1,0:T(8,128)S(1)}, f32[1,5,8,8,128]{4,3,2,1,0:T(8,128)}, u32[]{:S(2)}) copy-start(f32[1,5,8,8,128]{4,3,2,1,0:T(8,128)} %param.7) | copy-start | bytes 491524
  0.0 36.0 %copy-start.2 = (s32[1,1,1,1024]{3,2,1,0:T(1,128)S(1)}, s32[1,1,1,1024]{3,2,1,0:T(1,128)}, u32[]{:S(2)}) copy-start(s32[1,1,1,1024]{3,2,1,0:T(1,128)} %param.9) | copy-start | bytes 12292
  2.0 37.0 %copy-start.3 = (f32[1,1,1,1024]{3,2,1,0:T(1,128)S(1)}, f32[1,1,1,1024]{3,2,1,0:T(1,128)}, u32[]{:S(2)}) copy-start(f32[1,1,1,1024]{3,2,1,0:T(1,128)} %param.12) | copy-start | bytes 12292
  10.8 39.7 %all-to-all-start = ((s32[1,128,20]{2,0,1:T(1,128)}), s32[1,128,20]{2,0,1:T(1,128)S(1)}, u32[]{:S(2)}, u32[]{:S(2)}) async-start(s32[1,128,20]{2,0,1:T(1,128)} %bitcast.26), calls=%async_computation | async-start | bytes 131072 | tf_op jit(solution)/shard_map/all_to_all | solution.py:112
  30.7 72.8 %collective-permute-start.1 = (f32[11,3,8,128]{3,2,1,0:T(8,128)}, f32[11,3,8,128]{3,2,1,0:T(8,128)S(1)}, u32[]{:S(2)}, u32[]{:S(2)}) collective-permute-start(f32[11,3,8,128]{3,2,1,0:T(8,128)} %get-tuple-element.18), channel_id=1, source_target_pairs={{4,0},{8,4},{12,8},{16,12},{20,16},{24,20},{28,24},{32,28},{36,32}... | collective-permute-start | bytes 405512 | tf_op jit(solution)/shard_map/ppermute | solution.py:19
  32.8 70.7 %collective-permute-start = (f32[11,3,8,128]{3,2,1,0:T(8,128)S(1)}, f32[11,3,8,128]{3,2,1,0:T(8,128)S(1)}, u32[]{:S(2)}, u32[]{:S(2)}) collective-permute-start(f32[11,3,8,128]{3,2,1,0:T(8,128)S(1)} %get-tuple-element.17), channel_id=1, source_target_pairs={{0,4},{4,8},{8,12},{12,16},{16,20},{20,24},{24,28},{28,32},{32,36}... | collective-permute-start | bytes 405512 | tf_op jit(solution)/shard_map/ppermute | solution.py:18
  50.5 60.0 %all-to-all-start.1 = ((f32[5,128,20]{2,0,1:T(8,128)}), f32[5,128,20]{2,0,1:T(8,128)S(1)}, u32[]{:S(2)}, u32[]{:S(2)}) async-start(f32[5,128,20]{2,0,1:T(8,128)} %copy.22), calls=%async_computation.1 | async-start | bytes 1048576 | tf_op jit(solution)/shard_map/all_to_all | solution.py:111
  104.5 98.0 %collective-permute-start.3 = (f32[11,14,3,128]{3,2,1,0:T(4,128)}, f32[11,14,3,128]{3,2,1,0:T(4,128)S(1)}, u32[]{:S(2)}, u32[]{:S(2)}) collective-permute-start(f32[11,14,3,128]{3,2,1,0:T(4,128)} %get-tuple-element.16), channel_id=1, source_target_pairs={{1,0},{2,1},{3,2},{5,4},{6,5},{7,6},{9,8},{10,9},{11,10},{13,12},{... | collective-permute-start | bytes 709640 | tf_op jit(solution)/shard_map/ppermute | solution.py:19
  106.7 95.8 %collective-permute-start.2 = (f32[11,14,3,128]{3,2,1,0:T(4,128)}, f32[11,14,3,128]{3,2,1,0:T(4,128)S(1)}, u32[]{:S(2)}, u32[]{:S(2)}) collective-permute-start(f32[11,14,3,128]{3,2,1,0:T(4,128)} %get-tuple-element.15), channel_id=1, source_target_pairs={{0,1},{1,2},{2,3},{4,5},{5,6},{6,7},{8,9},{9,10},{10,11},{12,13},{... | collective-permute-start | bytes 709640 | tf_op jit(solution)/shard_map/ppermute | solution.py:18
where the time goes:
time: 205 us
  other arithmetic  87.6 us (43%)
  starting transfers between devices  52.5 us (26%)
  blocking collectives  44.9 us (22%)
  local copies, waits for them, and re-layouts  18.7 us (9%)
    scatter-add x1, other arithmetic, local(): source = source.at[:, merged_targets[0]].add(merged_values).reshape(chann...  66.5 us
    all_gather x1, blocking collectives, local(): lax.all_gather(tile_targets, 'sec', axis=1, tiled=True)  27.9 us
    all_to_all x1, starting transfers between devices, local(): lax.all_to_all(packed_values, ('gx', 'gy'), split_axis=1, concat_axis=1,...  23.5 us
    all_to_all x1, starting transfers between devices, local(): lax.all_to_all(packed_targets, ('gx', 'gy'), split_axis=1, concat_axis=1,...  18.3 us
    all_gather x1, blocking collectives, local(): lax.all_gather(tile_values, 'sec', axis=1, tiled=True)  17 us
    scatter x1, other arithmetic, local(): jnp.zeros((channels, buffer_width), jnp.float32).at[:, position]  9.7 us
    unnamed x11, local copies, waits for them, and re-layouts  7.16 us
    ppermute x2, starting transfers between devices, extended(): before = lax.ppermute(last, axis, up)  6.37 us
  transfers between devices with their start and end apart: 6, of which 0 were waited for; matrix products, arithmetic and copies ran while one was open for 46% of the time, Pallas kernels for 0%

commit v1 on v0

--- a/solution.py
+++ b/solution.py
@@ -113,7 +113,9 @@
     )
     merged_values, merged_targets = (
         lax.all_gather(tile_values, "sec", axis=1, tiled=True),
-        lax.all_gather(tile_targets, "sec", axis=1, tiled=True),
+        jnp.concatenate(
+            lax.all_to_all(jnp.stack([tile_targets] * lax.axis_size("sec")), "sec", 0, 0), axis=1
+        ),
     )
     source = jnp.zeros((channels, rows_x * rows_y * depth_cells), jnp.float32)
     source = (

time: 205 us -> 228 us (1.11)
  the two profiles are of different devices: /device:TPU:91 before, /device:TPU:1 now
where the time goes in v1:
time: 228 us; the launch traced here: 227 us
  other arithmetic  87.1 us (38%)
  starting transfers between devices  63.3 us (28%)
  waiting for transfers between devices  36.5 us (16%)
  blocking collectives  19.7 us (9%)
  local copies, waits for them, and re-layouts  19.2 us (8%)
    scatter-add x1, other arithmetic, local(): source = source.at[:, merged_targets[0]].add(merged_values).reshape(chann...  66.6 us
    all_to_all x1, waiting for transfers between devices, local(): lax.all_to_all(packed_values, ('gx', 'gy'), split_axis=1, concat_axis=1,...  30.6 us
    all_to_all x1, starting transfers between devices, local(): lax.all_to_all(packed_values, ('gx', 'gy'), split_axis=1, concat_axis=1,...  23.3 us
    all_to_all x1, starting transfers between devices, local(): lax.all_to_all(packed_targets, ('gx', 'gy'), split_axis=1, concat_axis=1,...  20.4 us
    all_gather x1, blocking collectives, local(): lax.all_gather(tile_values, 'sec', axis=1, tiled=True)  19.7 us
    scatter x1, other arithmetic, local(): jnp.zeros((channels, buffer_width), jnp.float32).at[:, position]  9.69 us
    all_to_all x1, starting transfers between devices, local(): lax.all_to_all(jnp.stack([tile_targets] * lax.axis_size('sec')), 'sec', 0...  9.08 us
    ppermute x2, starting transfers between devices, extended(): before = lax.ppermute(last, axis, up)  8 us
  transfers between devices with their start and end apart: 7, of which 2 were waited for; matrix products, arithmetic and copies ran while one was open for 41% of the time, Pallas kernels for 0%

profile of v1, /device:TPU:1, one launch (start us, length us, event | category | flops | bytes accessed | tf_op | source)
XLA Modules:
  0.0 226.9 jit_solution(647334463072322879)
XLA Ops:
  0.0 0.8 copy.17
  2.1 1.2 fusion.4
  3.3 0.7 compare_select_fusion.2
  4.0 0.7 and_reduce_fusion
  4.8 0.7 fusion.72
  5.6 4.5 %scatter_custom_fusion.2 = s32[2560]{0:T(1024)S(1)} fusion(s32[1024]{0:T(1024)S(1)} %broadcast_select_fusion.3, s32[1024]{0:T(1024)} %bitcast.146, s32[]{:T(128)} %constant.27.clone.1), kind=kCustom, calls=%fused_computation.167 | custom fusion | bytes 10752
  10.0 0.7 all_to_all.17
  10.8 20.4 %all-to-all-start = ((s32[1,128,20]{2,0,1:T(1,128)}), s32[1,128,20]{2,0,1:T(1,128)S(1)}, u32[]{:S(2)}, u32[]{:S(2)}) async-start(s32[1,128,20]{2,0,1:T(1,128)} %bitcast.26), calls=%async_computation | async-start | bytes 131072 | tf_op jit(solution)/shard_map/all_to_all | solution.py:112
  31.2 1.0 pad_maximum_fusion.4
  32.1 1.3 collective-permute-start.1
  33.4 4.0 %collective-permute-start = (f32[11,3,8,128]{3,2,1,0:T(8,128)S(1)}, f32[11,3,8,128]{3,2,1,0:T(8,128)S(1)}, u32[]{:S(2)}, u32[]{:S(2)}) collective-permute-start(f32[11,3,8,128]{3,2,1,0:T(8,128)S(1)} %get-tuple-element.17), channel_id=1, source_target_pairs={{0,4},{4,8},{8,12},{12,16},{16,20},{20,24},{24,28},{28,32},{32,36}... | collective-permute-start | bytes 405512 | tf_op jit(solution)/shard_map/ppermute | solution.py:18
  37.8 2.7 %copy.20 = f32[1,5,8,8,128]{1,4,3,2,0:T(8,128)} copy(f32[1,5,8,8,128]{4,3,2,1,0:T(8,128)S(1)} %copy-done) | data formatting | bytes 327680 | tf_op args[0]
  40.5 9.7 %scatter_custom_fusion = f32[5,2560]{0,1:T(8,128)S(1)} fusion(s32[1024]{0:T(1024)S(1)} %bitcast.142, f32[]{:T(128)} %constant.32.clone.1, f32[1024]{0:T(1024)S(1)} %bitcast.145, f32[5,8192]{0,1:T(8,128)} %bitcast.135, s32[1024]{0:T(1024)S(1)} %broadcast_clamp_fusion), kind=kCustom, calls=%fused_computation.7 | custom fusion | flops 5120 | bytes 223236 | tf_op jit(solution)/shard_map/scatter | solution.py:105
  50.2 0.4 copy.21
  51.0 1.0 copy.22
  52.0 0.5 broadcast.295
  52.5 0.8 reduce.7
  53.4 0.6 stack.32
  54.0 9.1 %all-to-all-start.1 = ((s32[4,1,2560]{2,1,0:T(1,128)}), s32[4,1,2560]{2,1,0:T(1,128)S(1)}, u32[]{:S(2)}, u32[]{:S(2)}) async-start(s32[4,1,2560]{2,1,0:T(1,128)} %stack.32), calls=%async_computation.1 | async-start | bytes 81920 | tf_op jit(solution)/shard_map/all_to_all | solution.py:117
  63.2 0.9 fusion.80
  64.1 1.3 collective-permute-start.3
  65.4 4.0 %collective-permute-start.2 = (f32[11,14,3,128]{3,2,1,0:T(4,128)}, f32[11,14,3,128]{3,2,1,0:T(4,128)S(1)}, u32[]{:S(2)}, u32[]{:S(2)}) collective-permute-start(f32[11,14,3,128]{3,2,1,0:T(4,128)} %get-tuple-element.15), channel_id=1, source_target_pairs={{0,1},{1,2},{2,3},{4,5},{5,6},{6,7},{8,9},{9,10},{10,11},{12,13},{... | collective-permute-start | bytes 709640 | tf_op jit(solution)/shard_map/ppermute | solution.py:18
  69.9 5.9 %all-to-all-done.1 = s32[4,1,2560]{2,1,0:T(1,128)S(1)} async-done(((s32[4,1,2560]{2,1,0:T(1,128)}), s32[4,1,2560]{2,1,0:T(1,128)S(1)}, u32[]{:S(2)}, u32[]{:S(2)}) %all-to-all-start.1) | async-done | bytes 40992 | tf_op jit(solution)/shard_map/all_to_all | solution.py:117
  75.7 23.3 %all-to-all-start.2 = ((f32[5,128,20]{2,0,1:T(8,128)}), f32[5,128,20]{2,0,1:T(8,128)S(1)}, u32[]{:S(2)}, u32[]{:S(2)}) async-start(f32[5,128,20]{2,0,1:T(8,128)} %copy.22), calls=%async_computation.2 | async-start | bytes 1048576 | tf_op jit(solution)/shard_map/all_to_all | solution.py:111
  99.1 30.6 %all-to-all-done.2 = f32[5,128,20]{2,0,1:T(8,128)S(1)} async-done(((f32[5,128,20]{2,0,1:T(8,128)}), f32[5,128,20]{2,0,1:T(8,128)S(1)}, u32[]{:S(2)}, u32[]{:S(2)}) %all-to-all-start.2) | async-done | bytes 51232 | tf_op jit(solution)/shard_map/all_to_all | solution.py:111
  130.0 19.7 %all_gather.3 = f32[5,10240]{1,0:T(8,128)S(1)} all-gather(f32[5,2560]{1,0:T(8,128)S(1)} %all_to_all.22), channel_id=1, replica_groups=mesh['sec'=4,'gx'=32,'gy'=4] {'sec'}, dimensions={1}, use_global_device_ids=true | all-gather | bytes 256000 | tf_op jit(solution)/shard_map/all_gather | solution.py:115
  149.6 3.1 %copy.24 = f32[10240,5]{1,0:T(8,128)} copy(f32[10240,5]{0,1:T(8,128)S(1)} %bitcast.137) | data formatting | bytes 409600 | tf_op jit(solution)/shard_map/all_gather | solution.py:115
  152.8 66.6 %scatter_custom_fusion.1 = f32[5,8192]{0,1:T(8,128)} fusion(s32[10240]{0:T(1024)S(1)} %bitcast.139, f32[10240,5]{1,0:T(8,128)} %copy.24, f32[]{:T(128)} %constant.32.clone.1), kind=kCustom, calls=%fused_computation.5 | custom fusion | flops 51200 | bytes 164352 | tf_op jit(solution)/shard_map/scatter-add | solution.py:123
  219.4 2.3 %broadcast_select_fusion = f32[5,8192]{0,1:T(8,128)} fusion(f32[5,8192]{0,1:T(8,128)} %scatter_custom_fusion.1, pred[]{:T(512)S(6)} %eq.28), kind=kLoop, calls=%fused_computation.4 | loop fusion | flops 40960 | bytes 327681 | tf_op jit(solution)/shard_map/jit(_where)/select_n | solution.py:127
  221.7 2.9 %copy.25 = f32[1,5,8,8,128]{4,3,2,1,0:T(8,128)S(1)} copy(f32[1,5,8,8,128]{1,4,3,2,0:T(8,128)} %bitcast.136) | data formatting | bytes 327680 | tf_op jit(solution)/shard_map/jit(_where)/select_n | solution.py:127
  225.4 0.7 add_add_fusion
  226.2 0.7 multiply_add_fusion
  (63 shorter events, 2.9 us)
Async XLA Ops:
  0.0 37.5 %copy-start.1 = (f32[1,6,8,8,128]{4,3,2,1,0:T(8,128)S(1)}, f32[1,6,8,8,128]{4,3,2,1,0:T(8,128)}, u32[]{:S(2)}) copy-start(f32[1,6,8,8,128]{4,3,2,1,0:T(8,128)} %param.8) | copy-start | bytes 589828
  0.0 37.5 %copy-start = (f32[1,5,8,8,128]{4,3,2,1,0:T(8,128)S(1)}, f32[1,5,8,8,128]{4,3,2,1,0:T(8,128)}, u32[]{:S(2)}) copy-start(f32[1,5,8,8,128]{4,3,2,1,0:T(8,128)} %param.7) | copy-start | bytes 491524
  0.0 37.5 %copy-start.2 = (s32[1,1,1,1024]{3,2,1,0:T(1,128)S(1)}, s32[1,1,1,1024]{3,2,1,0:T(1,128)}, u32[]{:S(2)}) copy-start(s32[1,1,1,1024]{3,2,1,0:T(1,128)} %param.9) | copy-start | bytes 12292
  2.0 38.5 %copy-start.3 = (f32[1,1,1,1024]{3,2,1,0:T(1,128)S(1)}, f32[1,1,1,1024]{3,2,1,0:T(1,128)}, u32[]{:S(2)}) copy-start(f32[1,1,1,1024]{3,2,1,0:T(1,128)} %param.12) | copy-start | bytes 12292
  10.8 41.2 %all-to-all-start = ((s32[1,128,20]{2,0,1:T(1,128)}), s32[1,128,20]{2,0,1:T(1,128)S(1)}, u32[]{:S(2)}, u32[]{:S(2)}) async-start(s32[1,128,20]{2,0,1:T(1,128)} %bitcast.26), calls=%async_computation | async-start | bytes 131072 | tf_op jit(solution)/shard_map/all_to_all | solution.py:112
  32.1 31.0 %collective-permute-start.1 = (f32[11,3,8,128]{3,2,1,0:T(8,128)S(1)}, f32[11,3,8,128]{3,2,1,0:T(8,128)S(1)}, u32[]{:S(2)}, u32[]{:S(2)}) collective-permute-start(f32[11,3,8,128]{3,2,1,0:T(8,128)S(1)} %get-tuple-element.18), channel_id=1, source_target_pairs={{4,0},{8,4},{12,8},{16,12},{20,16},{24,20},{28,24},{32,28},{36,32}... | collective-permute-start | bytes 405512 | tf_op jit(solution)/shard_map/ppermute | solution.py:19
  33.4 29.7 %collective-permute-start = (f32[11,3,8,128]{3,2,1,0:T(8,128)S(1)}, f32[11,3,8,128]{3,2,1,0:T(8,128)S(1)}, u32[]{:S(2)}, u32[]{:S(2)}) collective-permute-start(f32[11,3,8,128]{3,2,1,0:T(8,128)S(1)} %get-tuple-element.17), channel_id=1, source_target_pairs={{0,4},{4,8},{8,12},{12,16},{16,20},{20,24},{24,28},{28,32},{32,36}... | collective-permute-start | bytes 405512 | tf_op jit(solution)/shard_map/ppermute | solution.py:18
  54.0 21.7 %all-to-all-start.1 = ((s32[4,1,2560]{2,1,0:T(1,128)}), s32[4,1,2560]{2,1,0:T(1,128)S(1)}, u32[]{:S(2)}, u32[]{:S(2)}) async-start(s32[4,1,2560]{2,1,0:T(1,128)} %stack.32), calls=%async_computation.1 | async-start | bytes 81920 | tf_op jit(solution)/shard_map/all_to_all | solution.py:117
  64.1 160.5 %collective-permute-start.3 = (f32[11,14,3,128]{3,2,1,0:T(4,128)}, f32[11,14,3,128]{3,2,1,0:T(4,128)S(1)}, u32[]{:S(2)}, u32[]{:S(2)}) collective-permute-start(f32[11,14,3,128]{3,2,1,0:T(4,128)} %get-tuple-element.16), channel_id=1, source_target_pairs={{1,0},{2,1},{3,2},{5,4},{6,5},{7,6},{9,8},{10,9},{11,10},{13,12},{... | collective-permute-start | bytes 709640 | tf_op jit(solution)/shard_map/ppermute | solution.py:19
  65.4 159.2 %collective-permute-start.2 = (f32[11,14,3,128]{3,2,1,0:T(4,128)}, f32[11,14,3,128]{3,2,1,0:T(4,128)S(1)}, u32[]{:S(2)}, u32[]{:S(2)}) collective-permute-start(f32[11,14,3,128]{3,2,1,0:T(4,128)} %get-tuple-element.15), channel_id=1, source_target_pairs={{0,1},{1,2},{2,3},{4,5},{5,6},{6,7},{8,9},{9,10},{10,11},{12,13},{... | collective-permute-start | bytes 709640 | tf_op jit(solution)/shard_map/ppermute | solution.py:18
  75.7 54.0 %all-to-all-start.2 = ((f32[5,128,20]{2,0,1:T(8,128)}), f32[5,128,20]{2,0,1:T(8,128)S(1)}, u32[]{:S(2)}, u32[]{:S(2)}) async-start(f32[5,128,20]{2,0,1:T(8,128)} %copy.22), calls=%async_computation.2 | async-start | bytes 1048576 | tf_op jit(solution)/shard_map/all_to_all | solution.py:111
